TPU v7x, 32 devices: a whole 2x2x4 slice. The times are simulated.
32 devices in a mesh: span: 4 (over y, x), seq: 8 (over z, core).
Axes of the slice: x: 2, y: 2, z: 4, core: 2. Of those that a mesh axis runs over, the one named last changes fastest.
Arguments:
- hidden_in: bfloat16 [1024, 6144], P(('span', 'seq')), may hold values from -6 to 6
- qkv_weight: bfloat16 [6144, 3, 4096], P(None, None, 'seq'), may hold values from -0.078125 to 0.078125
- out_weight: bfloat16 [4096, 6144], P('seq'), may hold values from -0.09375 to 0.09375
- mod_table: bfloat16 [16, 2, 6144], replicated, may hold values from -1.5 to 9
- noise_level: int32 [4], replicated, may hold values from 0 to 15
- range_lo: int32 [4, 4], replicated, may hold values from 0 to 127
- range_len: int32 [4, 4], replicated, may hold values from 1 to 128
Outputs:
- hidden_out: bfloat16 [1024, 6144], P(('span', 'seq'))
Inputs may be any that keep to these rules, and one draw needn't show every extreme that they name: Only entries whose key span comes before the query span are read; range_lo + range_len stays below 256.
All inputs are finite; a program needn't handle non-finite values.
Results may differ from a plain program's by a relative error of at most 0.015.
The roundings to bfloat16 on the way count: a program that leaves them out, or rounds other values in their place, can miss the bound.
Values may be sent and summed in bfloat16 or wider, within the bound.
A program may use at most 128 MiB of HBM per device.

v0:
```python
import math

import jax
import jax.numpy as jnp
from jax import lax
from jax.sharding import PartitionSpec as P

HD = 128


def local(hidden_in, qkv_weight, out_weight, mod_table, noise_level, range_lo, range_len):
    span_id = lax.axis_index("span")
    span_count = lax.axis_size("span")
    span_range = jnp.arange(span_count, dtype=jnp.int32)
    level_here = jnp.sum(jnp.where(span_range == span_id, noise_level, 0))
    picker = (jnp.arange(mod_table.shape[0], dtype=jnp.int32) == level_here).astype(jnp.float32)
    modulation = jnp.einsum("l,lsd->sd", picker, mod_table.astype(jnp.float32))
    xfloat = hidden_in.astype(jnp.float32)
    row_mean = jnp.mean(xfloat, axis=-1, keepdims=True)
    row_var = jnp.mean((xfloat - row_mean) ** 2, axis=-1, keepdims=True)
    normed = (
        (xfloat - row_mean) * lax.rsqrt(row_var + 1e-06) * (1.0 + modulation[0]) + modulation[1]
    ).astype(jnp.bfloat16)
    width_dev = qkv_weight.shape[2]
    weights_flat = qkv_weight.reshape(qkv_weight.shape[0], 3 * width_dev)
    projected = jnp.dot(
        lax.all_gather(normed, "seq", axis=0, tiled=True),
        weights_flat,
        preferred_element_type=jnp.float32,
    ).astype(jnp.bfloat16)
    span_tok = projected.shape[0]
    heads_dev = width_dev // HD
    queries = projected[:, :width_dev].reshape(span_tok, heads_dev, HD)
    stacked = jnp.stack((projected[:, width_dev : 2 * width_dev], projected[:, 2 * width_dev :]))
    lo_mine = jnp.sum(jnp.where(span_range[:, None] == span_id, range_lo, 0), axis=0)
    len_mine = jnp.sum(jnp.where(span_range[:, None] == span_id, range_len, 0), axis=0)
    scale = HD ** (-0.5)

    def attend_block(running, key_block, value_block, key_span, offset):
        row_max, denominator, weighted = running
        key_count = key_block.shape[0]
        onehot = key_span[:, None] == span_range[None, :]
        lo_key = jnp.sum(jnp.where(onehot, lo_mine[None, :], 0), axis=1)
        len_key = jnp.sum(jnp.where(onehot, len_mine[None, :], 0), axis=1)
        visible = (key_span == span_id) | (key_span < span_id) & (offset >= lo_key) & (
            offset < lo_key + len_key
        )
        scores = (
            jnp.einsum(
                "qhd,khd->hqk",
                queries,
                key_block.reshape(key_count, heads_dev, HD),
                preferred_element_type=jnp.float32,
            )
            * scale
        )
        masked = jnp.where(visible[None, None, :], scores, -1e30)
        new_max = jnp.maximum(row_max, jnp.max(masked, axis=-1))
        weights = jnp.where(visible[None, None, :], jnp.exp(scores - new_max[..., None]), 0.0)
        factor = jnp.exp(row_max - new_max)
        denominator = denominator * factor + jnp.sum(weights, axis=-1)
        weighted = weighted * factor[..., None] + jnp.einsum(
            "hqk,khd->hqd",
            weights.astype(jnp.bfloat16),
            value_block.reshape(key_count, heads_dev, HD),
            preferred_element_type=jnp.float32,
        )
        return (new_max, denominator, weighted)

    initial = (
        jnp.full((heads_dev, span_tok), -1e30, jnp.float32),
        jnp.zeros((heads_dev, span_tok), jnp.float32),
        jnp.zeros((heads_dev, span_tok, HD), jnp.float32),
    )
    pieces_in = lax.all_gather(stacked, "span", axis=1, tiled=True)
    key_count = pieces_in.shape[1]
    block_rows = math.gcd(key_count, 512)

    def inner(carried, block_index):
        first_row = block_index * block_rows
        keys_here = lax.dynamic_slice_in_dim(pieces_in[0], first_row, block_rows, 0)
        values_here = lax.dynamic_slice_in_dim(pieces_in[1], first_row, block_rows, 0)
        positions = first_row + jnp.arange(block_rows, dtype=jnp.int32)
        key_span = positions // span_tok
        offset = positions - key_span * span_tok
        return (attend_block(carried, keys_here, values_here, key_span, offset), None)

    def work(carried):
        return lax.scan(inner, carried, jnp.arange(key_count // block_rows, dtype=jnp.int32))[0]

    def keep(carried):
        return carried

    running = lax.cond(jnp.int32(0) < (span_id + 1) * span_tok, work, keep, initial)
    attended = (running[2] / running[1][..., None]).astype(jnp.bfloat16)
    attended = attended.transpose(1, 0, 2).reshape(span_tok, width_dev)
    summed = lax.psum_scatter(
        jnp.dot(attended, out_weight, preferred_element_type=jnp.float32).astype(jnp.bfloat16),
        "seq",
        scatter_dimension=0,
        tiled=True,
    ).astype(jnp.float32)
    return (xfloat + summed).astype(jnp.bfloat16)


def solution(mesh):
    return jax.shard_map(
        local,
        mesh=mesh,
        in_specs=(
            P(("span", "seq"), None),
            P(None, None, "seq"),
            P("seq", None),
            P(),
            P(),
            P(),
            P(),
        ),
        out_specs=P(("span", "seq"), None),
        check_vma=False,
    )
```

profile of v0, /device:TPU:0, one launch (start us, length us, event | category | flops | bytes accessed | tf_op | source)
XLA Modules:
  0.0 176.3 jit_solution(17646195648527358365)
XLA Ops:
  6.5 0.0 copy-start
  6.5 0.0 all-gather.3.cloned.1.call-start
  6.5 1.3 select_reduce_fusion.3
  7.9 0.0 copy-done
  7.9 1.0 fusion.21
  8.9 1.2 convert_reduce_fusion
  10.1 1.3 fusion.16
  11.4 2.0 %fusion.19 = bf16[32,6144]{1,0:T(8,128)(2,1)} fusion(bf16[32,6144]{1,0:T(8,128)(2,1)} %param.11, f32[6144]{0:T(1024)S(1)} %bitcast.54, f32[6144]{0:T(1024)S(1)} %bitcast.53, f32[32]{0:T(128)S(1)} %add_rsqrt_fusion, f32[32]{0:T(128)S(1)} %broadcast_multiply_fusion), kind=kLoop, calls=%fused_computation.47 | loop fusion | flops 1179648 | bytes 835840 | tf_op jit(solution)/shard_map/convert_element_type | solution.py:23
  13.3 0.0 all-gather.3.cloned.1.call-update
  13.4 0.0 all-gather.5.cloned.1.call-start
  13.4 23.7 %copy.23 = bf16[6144,3,512]{0,2,1:T(8,128)(2,1)} copy(bf16[6144,3,512]{2,0,1:T(8,128)(2,1)} %param.12) | data formatting | bytes 37748736 | tf_op args[1]
  37.2 17.4 %all-gather.3.cloned.1.call-done = bf16[256,6144]{1,0:T(8,128)(2,1)} async-done(((bf16[32,6144]{1,0:T(8,128)(2,1)}), bf16[256,6144]{1,0:T(8,128)(2,1)}) %all-gather.3.cloned.1.call-update) | async-done | bytes 3145744 | tf_op jit(solution)/shard_map/all_gather | solution.py:27
  54.5 9.9 %convolution_convert_fusion.1 = bf16[256,1536]{1,0:T(8,128)(2,1)S(1)} fusion(bf16[256,6144]{1,0:T(8,128)(2,1)} %all-gather.3.cloned.1.call-done, bf16[6144,1536]{0,1:T(8,128)(2,1)} %bitcast.48), kind=kOutput, calls=%fused_computation.38 | convolution fusion | flops 4832231424 | bytes 22806528 | tf_op jit(solution)/shard_map/dot_general | solution.py:26
  64.5 0.0 copy-start.4
  64.5 0.0 copy-start.5
  64.5 0.8 pad_maximum_fusion
  65.4 0.0 all-gather.5.cloned.1.call-update
  65.4 0.0 reduce-scatter.2.cloned.1.call-start
  65.5 34.3 %all-gather.5.cloned.1.call-done = bf16[2,1024,512]{2,1,0:T(8,128)(2,1)} async-done(((bf16[2,256,512]{2,1,0:T(8,128)(2,1)}), bf16[2,1024,512]{2,1,0:T(8,128)(2,1)}) %all-gather.5.cloned.1.call-update) | async-done | bytes 2097168 | tf_op jit(solution)/shard_map/all_gather | solution.py:75
  99.7 0.0 copy-done.4
  99.7 0.0 copy-done.5
  99.7 20.4 %conditional.1 = (f32[4,256]{1,0:T(4,128)}, f32[4,256,128]{1,2,0:T(8,128)}) conditional(s32[]{:T(128)} %convert_element_type.33, () %tuple.32, (pred[4]{0:T(512)(128)(4,1)S(1)}, s32[4,4]{1,0:T(4,128)S(1)}, s32[4,4]{1,0:T(4,128)S(1)}, bf16[256,1536]{1,0:T(8,128)(2,1)S(1)}, s32[]{:T(128)}, /*index=5*/s32[4]{0:T(128)S(1)}, ...), branch_computations={%region_3.4_spmd, %region_4.13_spmd} | conditional | flops 274631744 | bytes 27081352 | solution.py:94
  99.7 0.1 select_reduce_fusion.1
  99.8 3.9 %copy.25 = bf16[2,1024,512]{1,2,0:T(8,128)(2,1)} copy(bf16[2,1024,512]{2,1,0:T(8,128)(2,1)} %get-tuple-element.297) | data formatting | bytes 4194304 | tf_op jit(solution)/shard_map
  103.7 0.3 copy.24
  104.0 0.2 copy.22
  104.3 13.8 %while.22 = (s32[]{:T(128)}, f32[4,256]{1,0:T(4,128)S(1)}, f32[4,256]{1,0:T(4,128)}, f32[4,256,128]{2,1,0:T(8,128)}, s32[2]{0:T(128)S(1)}, /*index=5*/s32[]{:T(1...) while((s32[]{:T(128)}, f32[4,256]{1,0:T(4,128)S(1)}, ...), condition=%wide.region_12.12_spmd.clone, body=%wide.region_7.11_spmd.clone.sunk | while | flops 274631680 | bytes 19216716 | solution.py:89
  104.3 0.7 dynamic_slice.21
  105.6 0.1 fusion.45
  105.7 1.7 fusion.47
  107.4 0.1 constant_dynamic-slice_fusion.3
  107.5 0.6 select_reduce_fusion.5
  108.1 0.0 copy-start.2
  108.1 0.5 bitcast_reduce_fusion.2
  108.6 0.6 fusion.48
  109.2 0.0 copy-done.2
  109.2 0.8 convolution_add_fusion.2
  110.0 0.0 copy-start.3
  110.0 0.8 copy-done.3
  110.8 0.6 dynamic_slice.21
  112.1 0.1 fusion.45
  112.2 1.7 fusion.47
  114.0 0.1 constant_dynamic-slice_fusion.3
  114.1 0.6 select_reduce_fusion.5
  114.6 0.0 copy-start.2
  114.7 0.5 bitcast_reduce_fusion.2
  115.1 1.3 fusion.48
  116.4 0.0 copy-done.2
  116.4 0.8 convolution_add_fusion.2
  117.2 0.0 copy-start.3
  117.3 0.8 copy-done.3
  118.0 2.0 %copy.33 = f32[4,256,128]{1,2,0:T(8,128)} copy(f32[4,256,128]{2,1,0:T(8,128)} %get-tuple-element.217) | data formatting | bytes 1048576 | tf_op jit(solution)/shard_map/cond | solution.py:94
  120.1 1.1 divide_convert_fusion
  121.2 6.3 %convolution_convert_fusion = bf16[256,6144]{1,0:T(8,128)(2,1)} fusion(bf16[256,512]{0,1:T(8,128)(2,1)S(1)} %bitcast.50, bf16[512,6144]{1,0:T(8,128)(2,1)} %param.13), kind=kOutput, calls=%fused_computation.37 | convolution fusion | flops 1612185600 | bytes 9699328 | tf_op jit(solution)/shard_map/dot_general | solution.py:98
  127.5 0.0 copy-start.1
  127.5 0.0 reduce-scatter.2.cloned.1.call-update
  127.5 40.5 %reduce-scatter.2.cloned.1.call-done = bf16[32,6144]{1,0:T(8,128)(2,1)} async-done(((bf16[256,6144]{1,0:T(8,128)(2,1)}), bf16[32,6144]{1,0:T(8,128)(2,1)}) %reduce-scatter.2.cloned.1.call-update) | async-done | bytes 393232 | tf_op jit(solution)/shard_map/reduce_scatter | solution.py:97
  168.0 0.0 copy-done.1
  168.0 1.8 %fusion.20 = bf16[32,6144]{1,0:T(8,128)(2,1)} fusion(bf16[32,6144]{1,0:T(8,128)(2,1)S(1)} %copy-done.1, bf16[32,6144]{1,0:T(8,128)(2,1)} %reduce-scatter.2.cloned.1.call-done), kind=kLoop, calls=%fused_computation.48 | loop fusion | flops 786432 | bytes 1179648 | tf_op jit(solution)/shard_map/convert_element_type | solution.py:103
  (20 shorter events, 0.2 us)
Async XLA Ops:
  6.5 1.4 copy-start
  6.5 48.0 %all-gather.3.cloned.1.call-start = ((), (), s32[]{:S(2)}) async-start(), calls=%async_computation.1 | async-start | bytes 3538944 | tf_op jit(solution)/shard_map/all_gather | solution.py:27
  13.4 86.3 %all-gather.5.cloned.1.call-start = ((), (), s32[]{:S(2)}) async-start(), calls=%async_computation.2 | async-start | bytes 2621440 | tf_op jit(solution)/shard_map/all_gather | solution.py:75
  64.5 35.3 %copy-start.4 = (s32[4,4]{1,0:T(4,128)S(1)}, s32[4,4]{1,0:T(4,128)}, u32[]{:S(2)}) copy-start(s32[4,4]{1,0:T(4,128)} %param.16) | copy-start | bytes 196
  64.5 35.2 %copy-start.5 = (s32[4,4]{1,0:T(4,128)S(1)}, s32[4,4]{1,0:T(4,128)}, u32[]{:S(2)}) copy-start(s32[4,4]{1,0:T(4,128)} %param.17) | copy-start | bytes 196
  65.4 102.6 %reduce-scatter.2.cloned.1.call-start = ((), (), s32[]{:S(2)}) async-start(), calls=%async_computation.3 | async-start | bytes 3538944 | tf_op jit(solution)/shard_map/reduce_scatter | solution.py:97
  108.1 1.1 copy-start.2
  110.0 0.8 copy-start.3
  114.6 1.8 %copy-start.2 = (f32[4,256,128]{2,1,0:T(8,128)S(1)}, f32[4,256,128]{2,1,0:T(8,128)}, u32[]{:S(2)}) copy-start(f32[4,256,128]{2,1,0:T(8,128)} %get-tuple-element.442) | copy-start | bytes 1572868 | tf_op jit(solution)/shard_map/cond/branch_1_fun/while
  117.2 0.8 copy-start.3
  127.5 40.5 %copy-start.1 = (bf16[32,6144]{1,0:T(8,128)(2,1)S(1)}, bf16[32,6144]{1,0:T(8,128)(2,1)}, u32[]{:S(2)}) copy-start(bf16[32,6144]{1,0:T(8,128)(2,1)} %param.11) | copy-start | bytes 1179652
Sparse Core Ops, SparseCore 0:
  13.5 40.9 all-gather.2
  65.5 34.1 all-gather.4
  127.6 40.3 reduce-scatter.1
where the time goes:
time: 177 us; the launch traced here: 176 us
  waiting for transfers between devices  92.2 us (52%)
  local copies, waits for them, and re-layouts  36.8 us (21%)
  matrix products  19.9 us (11%)
  between operations  13.2 us (7%)
  other arithmetic  12.7 us (7%)
    reduce_scatter x1, waiting for transfers between devices, local(): lax.psum_scatter(jnp.dot(attended, out_weight, preferred_element_type=jnp...  40.5 us
    all_gather x1, waiting for transfers between devices, local(): pieces_in = lax.all_gather(stacked, 'span', axis=1, tiled=True)  34.3 us
    unnamed x9, local copies, waits for them, and re-layouts  23.8 us
    all_gather x1, waiting for transfers between devices, local(): lax.all_gather(normed, 'seq', axis=0, tiled=True)  17.4 us
    dot_general x1, matrix products, local(): jnp.dot(lax.all_gather(normed, 'seq', axis=0, tiled=True), weights_flat,...  9.94 us
    dot_general x1, matrix products, local(): jnp.dot(attended, out_weight, preferred_element_type=jnp.float32)  6.28 us
    another operation x2, local copies, waits for them, and re-layouts  4.21 us
  transfers between devices with their start and end apart: 3, of which 3 were waited for; matrix products, arithmetic and copies ran while one was open for 13% of the time, Pallas kernels for 0%

commit v1 on v0

v1 whole, which is shorter than its diff:
```python
import functools

import jax
import jax.numpy as jnp
from jax import lax
from jax.experimental import pallas as pl
from jax.experimental.pallas import tpu as pltpu
from jax.sharding import PartitionSpec as P

HD = 128
F32 = jnp.float32
BF16 = jnp.bfloat16
MESH = pl.DeviceIdType.MESH


def kernel(
    nspan, nseq,
    level_ref, lo_ref, len_ref, x_ref, mod_ref, w_hbm, wo_hbm, out_ref,
    w, wo, xg, proj, win_out, win_in, att, acc, mx, den, term, sib, from_low, from_high, fwd, total,
    w_sem, wo_sem,
    g_send_up, g_send_down, g_send_sib, g_recv_z, g_recv_sib,
    k_send, k_recv,
    s_send_z, s_send_sib, s_recv_low, s_recv_high, s_recv_sib,
):
    span = lax.axis_index("span")
    seq = lax.axis_index("seq")
    nz = nseq // 2
    z = seq // 2
    core = seq - 2 * z
    rows, width = x_ref.shape
    tok = rows * nseq
    chunk = 2 * rows
    wdev = w.shape[2]
    heads = wdev // HD
    half = tok // 2
    up, down, other = seq + 2, seq - 2, 2 * z + 1 - core
    has_up, has_down = z < nz - 1, z > 0

    loads = [pltpu.make_async_copy(w_hbm.at[p], w.at[p], w_sem.at[p]) for p in range(3)]
    for p in (1, 2, 0):
        loads[p].start()
    load_out = pltpu.make_async_copy(wo_hbm, wo, wo_sem)
    load_out.start()

    barrier = pltpu.get_barrier_semaphore()

    @pl.when(has_up)
    def _():
        pl.semaphore_signal(barrier, inc=1, device_id=(span, up), device_id_type=MESH)

    @pl.when(has_down)
    def _():
        pl.semaphore_signal(barrier, inc=1, device_id=(span, down), device_id_type=MESH)

    pl.semaphore_signal(barrier, inc=1, device_id=(span, other), device_id_type=MESH)

    def greet(i, carry):
        pl.semaphore_signal(
            barrier, inc=1, device_id=(lax.rem(span + i, nspan), seq), device_id_type=MESH
        )
        return carry

    lax.fori_loop(1, nspan, greet, 0)

    def block(index):
        return pl.ds(pl.multiple_of(index * rows, rows), rows)

    def chunk_rows(index):
        return pl.ds(pl.multiple_of(index * chunk, chunk), chunk)

    x = x_ref[...].astype(F32)
    mod = mod_ref[level_ref[span]].astype(F32)
    mean = jnp.mean(x, axis=-1, keepdims=True)
    centred = x - mean
    var = jnp.mean(centred * centred, axis=-1, keepdims=True)
    normed = centred * lax.rsqrt(var + 1e-06) * (1.0 + mod[0:1]) + mod[1:2]
    xg[block(seq), :] = normed.astype(BF16)

    pl.semaphore_wait(
        barrier, has_up.astype(jnp.int32) + has_down.astype(jnp.int32) + nspan
    )

    def g_copy(origin, target, send_sem, recv_sem):
        return pltpu.make_async_remote_copy(
            src_ref=xg.at[block(origin)], dst_ref=xg.at[block(origin)],
            send_sem=send_sem, recv_sem=recv_sem, device_id=(span, target), device_id_type=MESH,
        )

    def g_up(oz):
        return g_copy(2 * oz + core, up, g_send_up.at[oz], g_recv_z.at[oz])

    def g_down(oz):
        return g_copy(2 * oz + core, down, g_send_down.at[oz], g_recv_z.at[oz])

    def g_sib(oz):
        return g_copy(2 * oz + core, other, g_send_sib.at[oz], g_recv_sib.at[oz])

    def g_sib_in(oz):
        return g_copy(2 * oz + 1 - core, other, g_send_sib.at[oz], g_recv_sib.at[oz])

    def gather_step(k, carry):
        low, high = z - k, z + k

        @pl.when((k > 0) & (low >= 0))
        def _():
            g_up(low).wait_recv()

        @pl.when((low >= 0) & has_up)
        def _():
            g_up(low).start()

        @pl.when((k > 0) & (high < nz))
        def _():
            g_down(high).wait_recv()

        @pl.when((high < nz) & has_down)
        def _():
            g_down(high).start()

        @pl.when(low >= 0)
        def _():
            g_sib(low).start()

        @pl.when((k > 0) & (high < nz))
        def _():
            g_sib(high).start()

        @pl.when(k == 0)
        def _():
            for p in range(3):
                loads[p].wait()

        def side(i, c):
            oz = jnp.where(i == 0, low, high)

            @pl.when(((i == 0) & (low >= 0)) | ((i == 1) & (k > 0) & (high < nz)))
            def _():
                g_sib_in(oz).wait_recv()

                def part(p, cc):
                    proj[p, chunk_rows(oz), :] = jnp.dot(
                        xg[chunk_rows(oz), :], w[p], preferred_element_type=F32
                    ).astype(BF16)
                    return cc

                lax.fori_loop(0, 3, part, 0)

            return c

        lax.fori_loop(0, 2, side, 0)
        return carry

    lax.fori_loop(0, nz, gather_step, 0)

    def k_copy(i):
        return pltpu.make_async_remote_copy(
            src_ref=win_out.at[i], dst_ref=win_in.at[span],
            send_sem=k_send.at[i], recv_sem=k_recv.at[span],
            device_id=(i, seq), device_id_type=MESH,
        )

    def k_copy_in(i):
        return pltpu.make_async_remote_copy(
            src_ref=win_out.at[i], dst_ref=win_in.at[i],
            send_sem=k_send.at[i], recv_sem=k_recv.at[i],
            device_id=(i, seq), device_id_type=MESH,
        )

    def send_window(i, carry):
        first = lo_ref[i, span]
        row = lax.broadcasted_iota(jnp.int32, (half, tok), 0)
        col = lax.broadcasted_iota(jnp.int32, (half, tok), 1)
        pick = jnp.where(col == row + first, 1.0, 0.0).astype(BF16)
        for p in range(2):
            win_out[i, p] = jnp.dot(pick, proj[p + 1], preferred_element_type=F32).astype(BF16)
        k_copy(i).start()
        return carry

    lax.fori_loop(span + 1, nspan, send_window, 0)

    scale = HD ** (-0.5)
    trans = (((1,), (1,)), ((), ()))
    for h in range(heads):
        cols = slice(h * HD, (h + 1) * HD)
        s = lax.dot_general(
            proj[0, :, cols], proj[1, :, cols], trans, preferred_element_type=F32
        ) * scale
        m = jnp.max(s, axis=-1, keepdims=True)
        e = jnp.exp(s - m)
        mx[h] = jnp.broadcast_to(m, (tok, HD))
        den[h] = jnp.broadcast_to(jnp.sum(e, axis=-1, keepdims=True), (tok, HD))
        acc[h] = jnp.dot(e.astype(BF16), proj[2, :, cols], preferred_element_type=F32)

    def see_window(j, carry):
        k_copy_in(j).wait_recv()
        seen = lax.broadcasted_iota(jnp.int32, (tok, half), 1) < len_ref[span, j]
        for h in range(heads):
            cols = slice(h * HD, (h + 1) * HD)
            s = lax.dot_general(
                proj[0, :, cols], win_in[j, 0, :, cols], trans, preferred_element_type=F32
            ) * scale
            s = jnp.where(seen, s, -1e30)
            old = mx[h]
            new = jnp.maximum(old, jnp.max(s, axis=-1, keepdims=True))
            e = jnp.where(seen, jnp.exp(s - new[:, 0:1]), 0.0)
            factor = jnp.exp(old - new)
            mx[h] = new
            den[h] = den[h] * factor + jnp.sum(e, axis=-1, keepdims=True)
            acc[h] = acc[h] * factor + jnp.dot(
                e.astype(BF16), win_in[j, 1, :, cols], preferred_element_type=F32
            )
        return carry

    lax.fori_loop(0, span, see_window, 0)
    for h in range(heads):
        att[:, h * HD:(h + 1) * HD] = (acc[h] / den[h]).astype(BF16)

    load_out.wait()

    def s_sib(d):
        return pltpu.make_async_remote_copy(
            src_ref=term.at[block(2 * d + 1 - core)], dst_ref=sib.at[d],
            send_sem=s_send_sib.at[d], recv_sem=s_recv_sib.at[d],
            device_id=(span, other), device_id_type=MESH,
        )

    def project(i, carry):
        d = jnp.where(z >= nz // 2, i, nz - 1 - i)
        term[chunk_rows(d), :] = jnp.dot(
            att[chunk_rows(d), :], wo[...], preferred_element_type=F32
        ).astype(BF16)
        s_sib(d).start()
        return carry

    lax.fori_loop(0, nz, project, 0)

    def s_up(d):
        return pltpu.make_async_remote_copy(
            src_ref=fwd.at[d], dst_ref=from_low.at[d],
            send_sem=s_send_z.at[d], recv_sem=s_recv_low.at[d],
            device_id=(span, up), device_id_type=MESH,
        )

    def s_down(d):
        return pltpu.make_async_remote_copy(
            src_ref=fwd.at[d], dst_ref=from_high.at[d],
            send_sem=s_send_z.at[d], recv_sem=s_recv_high.at[d],
            device_id=(span, down), device_id_type=MESH,
        )

    def pair(d):
        return term[block(2 * d + core), :].astype(F32) + sib[d].astype(F32)

    def scatter_step(t, carry):
        i = t - z
        d_up = nz - 1 - i

        @pl.when((i >= 0) & (d_up > z))
        def _():
            s_sib(d_up).wait_recv()

            @pl.when(has_down)
            def _():
                s_up(d_up).wait_recv()
                fwd[d_up] = (pair(d_up) + from_low[d_up].astype(F32)).astype(BF16)

            @pl.when(jnp.logical_not(has_down))
            def _():
                fwd[d_up] = pair(d_up).astype(BF16)

            s_up(d_up).start()

        d_down = t - (nz - 1 - z)

        @pl.when((d_down >= 0) & (d_down < z))
        def _():
            s_sib(d_down).wait_recv()

            @pl.when(has_up)
            def _():
                s_down(d_down).wait_recv()
                fwd[d_down] = (pair(d_down) + from_high[d_down].astype(F32)).astype(BF16)

            @pl.when(jnp.logical_not(has_up))
            def _():
                fwd[d_down] = pair(d_down).astype(BF16)

            s_down(d_down).start()

        return carry

    lax.fori_loop(0, nz - 1, scatter_step, 0)

    s_sib(z).wait_recv()
    total[...] = x_ref[...].astype(F32) + pair(z)

    @pl.when(has_down)
    def _():
        s_up(z).wait_recv()
        total[...] += from_low[z].astype(F32)

    @pl.when(has_up)
    def _():
        s_down(z).wait_recv()
        total[...] += from_high[z].astype(F32)

    out_ref[...] = total[...].astype(BF16)

    def drain(oz, carry):
        g_sib(oz).wait_send()
        s_sib(oz).wait_send()

        @pl.when((oz <= z) & has_up)
        def _():
            g_up(oz).wait_send()

        @pl.when((oz >= z) & has_down)
        def _():
            g_down(oz).wait_send()

        @pl.when(oz > z)
        def _():
            s_up(oz).wait_send()

        @pl.when(oz < z)
        def _():
            s_down(oz).wait_send()

        return carry

    lax.fori_loop(0, nz, drain, 0)

    def drain_window(i, carry):
        k_copy(i).wait_send()
        return carry

    lax.fori_loop(span + 1, nspan, drain_window, 0)


def local(nspan, nseq, hidden_in, qkv_weight, out_weight, mod_table, noise_level, range_lo, range_len):
    rows, width = hidden_in.shape
    wdev = qkv_weight.shape[2]
    tok = rows * nseq
    nz = nseq // 2
    heads = wdev // HD
    smem = pl.BlockSpec(memory_space=pltpu.SMEM)
    vmem = pl.BlockSpec(memory_space=pltpu.VMEM)
    hbm = pl.BlockSpec(memory_space=pl.ANY)
    dma = pltpu.SemaphoreType.DMA
    return pl.pallas_call(
        functools.partial(kernel, nspan, nseq),
        out_shape=jax.ShapeDtypeStruct((rows, width), BF16),
        in_specs=[smem, smem, smem, vmem, vmem, hbm, hbm],
        out_specs=vmem,
        scratch_shapes=[
            pltpu.VMEM((3, width, wdev), BF16),
            pltpu.VMEM((wdev, width), BF16),
            pltpu.VMEM((tok, width), BF16),
            pltpu.VMEM((3, tok, wdev), BF16),
            pltpu.VMEM((nspan, 2, tok // 2, wdev), BF16),
            pltpu.VMEM((nspan, 2, tok // 2, wdev), BF16),
            pltpu.VMEM((tok, wdev), BF16),
            pltpu.VMEM((heads, tok, HD), F32),
            pltpu.VMEM((heads, tok, HD), F32),
            pltpu.VMEM((heads, tok, HD), F32),
            pltpu.VMEM((tok, width), BF16),
            pltpu.VMEM((nz, rows, width), BF16),
            pltpu.VMEM((nz, rows, width), BF16),
            pltpu.VMEM((nz, rows, width), BF16),
            pltpu.VMEM((nz, rows, width), BF16),
            pltpu.VMEM((rows, width), F32),
            dma((3,)), dma(()),
            dma((nz,)), dma((nz,)), dma((nz,)), dma((nz,)), dma((nz,)),
            dma((nspan,)), dma((nspan,)),
            dma((nz,)), dma((nz,)), dma((nz,)), dma((nz,)), dma((nz,)),
        ],
        compiler_params=pltpu.CompilerParams(
            collective_id=0, has_side_effects=True, vmem_limit_bytes=58 * 1024 * 1024
        ),
    )(
        noise_level, range_lo, range_len, hidden_in, mod_table,
        qkv_weight.transpose(1, 0, 2), out_weight,
    )


def solution(mesh):
    return jax.shard_map(
        functools.partial(local, mesh.shape["span"], mesh.shape["seq"]),
        mesh=mesh,
        in_specs=(
            P(("span", "seq"), None),
            P(None, None, "seq"),
            P("seq", None),
            P(),
            P(),
            P(),
            P(),
        ),
        out_specs=P(("span", "seq"), None),
        check_vma=False,
    )
```

time: 177 us -> 93.3 us (0.53)
  the two profiles are of different devices: /device:TPU:0 before, /device:TPU:14 now
where the time goes in v1:
time: 93.3 us; the launch traced here: 93.2 us
  Pallas kernels  91.4 us (98%)
  local copies, waits for them, and re-layouts  1.77 us (2%)
    pallas_call x1, Pallas kernels, local(): pl.pallas_call(functools.partial(kernel, nspan, nseq), out_shape=jax.Shap...  91.4 us

profile of v1, /device:TPU:14, one launch (start us, length us, event | category | flops | bytes accessed | tf_op | source)
XLA Modules:
  0.0 93.2 jit_solution(1945803784509468015)
XLA Ops:
  0.0 91.4 %shard_map.73 = bf16[32,6144]{1,0:T(8,128)(2,1)} custom-call(s32[4]{0:T(128)} %level_ref.1, s32[4,4]{1,0:T(4,128)} %lo_ref.1, s32[4,4]{1,0:T(4,128)} %len_ref.1, bf16[32,6144]{1,0:T(8,128)(2,1)} %x_ref.1, bf16[16,2,6144]{2,1,0:T(2,128)(2,1)} %mod_ref.1, bf16[3,6144,512]{2,1,0:T(8,128)(2,1)} %bitcast.1, bf16[512,6144]{1,0:T(8,128)(2,1)} %wo_hbm.1), custom_call_target="tpu_custom_call" | custom-call | tf_op jit(solution)/shard_map/pallas_call | solution.py:350
  91.4 1.8 %copy.9 = bf16[32,6144]{1,0:T(8,128)(2,1)} copy(bf16[32,6144]{1,0:T(8,128)(2,1)} %shard_map.73) | data formatting | bytes 786432

commit v2 on v1

--- a/solution.py
+++ b/solution.py
@@ -80,50 +80,58 @@
         barrier, has_up.astype(jnp.int32) + has_down.astype(jnp.int32) + nspan
     )
 
-    def g_copy(origin, target, send_sem, recv_sem):
-        return pltpu.make_async_remote_copy(
-            src_ref=xg.at[block(origin)], dst_ref=xg.at[block(origin)],
+    def columns(part):
+        return slice(part * (width // 2), (part + 1) * (width // 2))
+
+    def g_copy(origin, part, target, send_sem, recv_sem):
+        return pltpu.make_async_remote_copy(
+            src_ref=xg.at[block(origin), columns(part)], dst_ref=xg.at[block(origin), columns(part)],
             send_sem=send_sem, recv_sem=recv_sem, device_id=(span, target), device_id_type=MESH,
         )
 
-    def g_up(oz):
-        return g_copy(2 * oz + core, up, g_send_up.at[oz], g_recv_z.at[oz])
-
-    def g_down(oz):
-        return g_copy(2 * oz + core, down, g_send_down.at[oz], g_recv_z.at[oz])
-
-    def g_sib(oz):
-        return g_copy(2 * oz + core, other, g_send_sib.at[oz], g_recv_sib.at[oz])
-
-    def g_sib_in(oz):
-        return g_copy(2 * oz + 1 - core, other, g_send_sib.at[oz], g_recv_sib.at[oz])
+    def g_up(oz, part):
+        at = 2 * oz + part
+        return g_copy(2 * oz + core, part, up, g_send_up.at[at], g_recv_z.at[at])
+
+    def g_down(oz, part):
+        at = 2 * oz + part
+        return g_copy(2 * oz + core, part, down, g_send_down.at[at], g_recv_z.at[at])
+
+    def g_sib(oz, part):
+        at = 2 * oz + part
+        return g_copy(2 * oz + core, part, other, g_send_sib.at[at], g_recv_sib.at[at])
+
+    def g_sib_in(oz, part):
+        at = 2 * oz + part
+        return g_copy(2 * oz + 1 - core, part, other, g_send_sib.at[at], g_recv_sib.at[at])
 
     def gather_step(k, carry):
         low, high = z - k, z + k
 
-        @pl.when((k > 0) & (low >= 0))
-        def _():
-            g_up(low).wait_recv()
-
-        @pl.when((low >= 0) & has_up)
-        def _():
-            g_up(low).start()
-
-        @pl.when((k > 0) & (high < nz))
-        def _():
-            g_down(high).wait_recv()
-
-        @pl.when((high < nz) & has_down)
-        def _():
-            g_down(high).start()
-
-        @pl.when(low >= 0)
-        def _():
-            g_sib(low).start()
-
-        @pl.when((k > 0) & (high < nz))
-        def _():
-            g_sib(high).start()
+        for half_at in range(2):
+            @pl.when((k > 0) & (low >= 0))
+            def _():
+                g_up(low, half_at).wait_recv()
+
+            @pl.when((low >= 0) & has_up)
+            def _():
+                g_up(low, half_at).start()
+
+            @pl.when((k > 0) & (high < nz))
+            def _():
+                g_down(high, half_at).wait_recv()
+
+            @pl.when((high < nz) & has_down)
+            def _():
+                g_down(high, half_at).start()
+
+            @pl.when(low >= 0)
+            def _():
+                g_sib(low, half_at).start()
+
+            @pl.when((k > 0) & (high < nz))
+            def _():
+                g_sib(high, half_at).start()
 
         @pl.when(k == 0)
         def _():
@@ -135,7 +143,8 @@
 
             @pl.when(((i == 0) & (low >= 0)) | ((i == 1) & (k > 0) & (high < nz)))
             def _():
-                g_sib_in(oz).wait_recv()
+                g_sib_in(oz, 0).wait_recv()
+                g_sib_in(oz, 1).wait_recv()
 
                 def part(p, cc):
                     proj[p, chunk_rows(oz), :] = jnp.dot(
@@ -191,29 +200,11 @@
         den[h] = jnp.broadcast_to(jnp.sum(e, axis=-1, keepdims=True), (tok, HD))
         acc[h] = jnp.dot(e.astype(BF16), proj[2, :, cols], preferred_element_type=F32)
 
-    def see_window(j, carry):
+    def await_window(j, carry):
         k_copy_in(j).wait_recv()
-        seen = lax.broadcasted_iota(jnp.int32, (tok, half), 1) < len_ref[span, j]
-        for h in range(heads):
-            cols = slice(h * HD, (h + 1) * HD)
-            s = lax.dot_general(
-                proj[0, :, cols], win_in[j, 0, :, cols], trans, preferred_element_type=F32
-            ) * scale
-            s = jnp.where(seen, s, -1e30)
-            old = mx[h]
-            new = jnp.maximum(old, jnp.max(s, axis=-1, keepdims=True))
-            e = jnp.where(seen, jnp.exp(s - new[:, 0:1]), 0.0)
-            factor = jnp.exp(old - new)
-            mx[h] = new
-            den[h] = den[h] * factor + jnp.sum(e, axis=-1, keepdims=True)
-            acc[h] = acc[h] * factor + jnp.dot(
-                e.astype(BF16), win_in[j, 1, :, cols], preferred_element_type=F32
-            )
-        return carry
-
-    lax.fori_loop(0, span, see_window, 0)
-    for h in range(heads):
-        att[:, h * HD:(h + 1) * HD] = (acc[h] / den[h]).astype(BF16)
+        return carry
+
+    lax.fori_loop(0, span, await_window, 0)
 
     load_out.wait()
 
@@ -224,107 +215,138 @@
             device_id=(span, other), device_id_type=MESH,
         )
 
-    def project(i, carry):
-        d = jnp.where(z >= nz // 2, i, nz - 1 - i)
-        term[chunk_rows(d), :] = jnp.dot(
-            att[chunk_rows(d), :], wo[...], preferred_element_type=F32
+    def project(d):
+        mine = chunk_rows(d)
+
+        def see_window(j, carry):
+            seen = lax.broadcasted_iota(jnp.int32, (chunk, half), 1) < len_ref[span, j]
+            for h in range(heads):
+                cols = slice(h * HD, (h + 1) * HD)
+                s = lax.dot_general(
+                    proj[0, mine, cols], win_in[j, 0, :, cols], trans,
+                    preferred_element_type=F32,
+                ) * scale
+                s = jnp.where(seen, s, -1e30)
+                old = mx[h, mine, :]
+                new = jnp.maximum(old, jnp.max(s, axis=-1, keepdims=True))
+                e = jnp.where(seen, jnp.exp(s - new[:, 0:1]), 0.0)
+                factor = jnp.exp(old - new)
+                mx[h, mine, :] = new
+                den[h, mine, :] = den[h, mine, :] * factor + jnp.sum(e, axis=-1, keepdims=True)
+                acc[h, mine, :] = acc[h, mine, :] * factor + jnp.dot(
+                    e.astype(BF16), win_in[j, 1, :, cols], preferred_element_type=F32
+                )
+            return carry
+
+        lax.fori_loop(0, span, see_window, 0)
+        for h in range(heads):
+            att[mine, h * HD:(h + 1) * HD] = (acc[h, mine, :] / den[h, mine, :]).astype(BF16)
+        term[mine, :] = jnp.dot(
+            att[mine, :], wo[...], preferred_element_type=F32
         ).astype(BF16)
         s_sib(d).start()
-        return carry
-
-    lax.fori_loop(0, nz, project, 0)
-
-    def s_up(d):
-        return pltpu.make_async_remote_copy(
-            src_ref=fwd.at[d], dst_ref=from_low.at[d],
-            send_sem=s_send_z.at[d], recv_sem=s_recv_low.at[d],
+
+    def s_up(d, part):
+        return pltpu.make_async_remote_copy(
+            src_ref=fwd.at[d, :, columns(part)], dst_ref=from_low.at[d, :, columns(part)],
+            send_sem=s_send_z.at[2 * d + part], recv_sem=s_recv_low.at[2 * d + part],
             device_id=(span, up), device_id_type=MESH,
         )
 
-    def s_down(d):
-        return pltpu.make_async_remote_copy(
-            src_ref=fwd.at[d], dst_ref=from_high.at[d],
-            send_sem=s_send_z.at[d], recv_sem=s_recv_high.at[d],
+    def s_down(d, part):
+        return pltpu.make_async_remote_copy(
+            src_ref=fwd.at[d, :, columns(part)], dst_ref=from_high.at[d, :, columns(part)],
+            send_sem=s_send_z.at[2 * d + part], recv_sem=s_recv_high.at[2 * d + part],
             device_id=(span, down), device_id_type=MESH,
         )
 
-    def pair(d):
-        return term[block(2 * d + core), :].astype(F32) + sib[d].astype(F32)
-
-    def scatter_step(t, carry):
+    def pair(d, cols=slice(None)):
+        return term[block(2 * d + core), cols].astype(F32) + sib[d, :, cols].astype(F32)
+
+    def pass_on(d, copy, arrived, more):
+        s_sib(d).wait_recv()
+        for part in range(2):
+            cols = columns(part)
+
+            @pl.when(more)
+            def _():
+                copy(d, part).wait_recv()
+                fwd[d, :, cols] = (pair(d, cols) + arrived[d, :, cols].astype(F32)).astype(BF16)
+
+            @pl.when(jnp.logical_not(more))
+            def _():
+                fwd[d, :, cols] = pair(d, cols).astype(BF16)
+
+            copy(d, part).start()
+
+    def scatter_step(t):
         i = t - z
         d_up = nz - 1 - i
 
         @pl.when((i >= 0) & (d_up > z))
         def _():
-            s_sib(d_up).wait_recv()
-
-            @pl.when(has_down)
-            def _():
-                s_up(d_up).wait_recv()
-                fwd[d_up] = (pair(d_up) + from_low[d_up].astype(F32)).astype(BF16)
-
-            @pl.when(jnp.logical_not(has_down))
-            def _():
-                fwd[d_up] = pair(d_up).astype(BF16)
-
-            s_up(d_up).start()
+            pass_on(d_up, s_up, from_low, has_down)
 
         d_down = t - (nz - 1 - z)
 
         @pl.when((d_down >= 0) & (d_down < z))
         def _():
-            s_sib(d_down).wait_recv()
-
-            @pl.when(has_up)
-            def _():
-                s_down(d_down).wait_recv()
-                fwd[d_down] = (pair(d_down) + from_high[d_down].astype(F32)).astype(BF16)
-
-            @pl.when(jnp.logical_not(has_up))
-            def _():
-                fwd[d_down] = pair(d_down).astype(BF16)
-
-            s_down(d_down).start()
-
-        return carry
-
-    lax.fori_loop(0, nz - 1, scatter_step, 0)
+            pass_on(d_down, s_down, from_high, has_up)
+
+    at_end = jnp.logical_not(has_up & has_down)
+
+    def step(u, carry):
+        @pl.when(u < nz)
+        def _():
+            project(jnp.where(z >= nz // 2, u, nz - 1 - u))
+
+        t = jnp.where(at_end, u, u - nz)
+
+        @pl.when((t >= 0) & (t < nz - 1))
+        def _():
+            scatter_step(t)
+
+        return carry
+
+    lax.fori_loop(0, 2 * nz - 1, step, 0)
 
     s_sib(z).wait_recv()
     total[...] = x_ref[...].astype(F32) + pair(z)
 
     @pl.when(has_down)
     def _():
-        s_up(z).wait_recv()
+        s_up(z, 0).wait_recv()
+        s_up(z, 1).wait_recv()
         total[...] += from_low[z].astype(F32)
 
     @pl.when(has_up)
     def _():
-        s_down(z).wait_recv()
+        s_down(z, 0).wait_recv()
+        s_down(z, 1).wait_recv()
         total[...] += from_high[z].astype(F32)
 
     out_ref[...] = total[...].astype(BF16)
 
     def drain(oz, carry):
-        g_sib(oz).wait_send()
         s_sib(oz).wait_send()
-
-        @pl.when((oz <= z) & has_up)
-        def _():
-            g_up(oz).wait_send()
-
-        @pl.when((oz >= z) & has_down)
-        def _():
-            g_down(oz).wait_send()
-
-        @pl.when(oz > z)
-        def _():
-            s_up(oz).wait_send()
-
-        @pl.when(oz < z)
-        def _():
-            s_down(oz).wait_send()
+        for part in range(2):
+            g_sib(oz, part).wait_send()
+
+            @pl.when((oz <= z) & has_up)
+            def _():
+                g_up(oz, part).wait_send()
+
+            @pl.when((oz >= z) & has_down)
+            def _():
+                g_down(oz, part).wait_send()
+
+            @pl.when(oz > z)
+            def _():
+                s_up(oz, part).wait_send()
+
+            @pl.when(oz < z)
+            def _():
+                s_down(oz, part).wait_send()
 
         return carry
 
@@ -370,9 +392,9 @@
             pltpu.VMEM((nz, rows, width), BF16),
             pltpu.VMEM((rows, width), F32),
             dma((3,)), dma(()),
-            dma((nz,)), dma((nz,)), dma((nz,)), dma((nz,)), dma((nz,)),
+            dma((2 * nz,)), dma((2 * nz,)), dma((2 * nz,)), dma((2 * nz,)), dma((2 * nz,)),
             dma((nspan,)), dma((nspan,)),
-            dma((nz,)), dma((nz,)), dma((nz,)), dma((nz,)), dma((nz,)),
+            dma((2 * nz,)), dma((nz,)), dma((2 * nz,)), dma((2 * nz,)), dma((nz,)),
         ],
         compiler_params=pltpu.CompilerParams(
             collective_id=0, has_side_effects=True, vmem_limit_bytes=58 * 1024 * 1024

time: 93.3 us -> 90.6 us (0.971)
  the two profiles are of different devices: /device:TPU:14 before, /device:TPU:7 now
where the time goes in v2:
time: 90.6 us; the launch traced here: 90.4 us
  Pallas kernels  88.6 us (98%)
  local copies, waits for them, and re-layouts  1.77 us (2%)
    pallas_call x1, Pallas kernels, local(): pl.pallas_call(functools.partial(kernel, nspan, nseq), out_shape=jax.Shap...  88.6 us

profile of v2, /device:TPU:7, one launch (start us, length us, event | category | flops | bytes accessed | tf_op | source)
XLA Modules:
  0.0 90.4 jit_solution(10759483168954265496)
XLA Ops:
  0.0 88.6 %shard_map.73 = bf16[32,6144]{1,0:T(8,128)(2,1)} custom-call(s32[4]{0:T(128)} %level_ref.1, s32[4,4]{1,0:T(4,128)} %lo_ref.1, s32[4,4]{1,0:T(4,128)} %len_ref.1, bf16[32,6144]{1,0:T(8,128)(2,1)} %x_ref.1, bf16[16,2,6144]{2,1,0:T(2,128)(2,1)} %mod_ref.1, bf16[3,6144,512]{2,1,0:T(8,128)(2,1)} %bitcast.1, bf16[512,6144]{1,0:T(8,128)(2,1)} %wo_hbm.1), custom_call_target="tpu_custom_call" | custom-call | tf_op jit(solution)/shard_map/pallas_call | solution.py:372
  88.6 1.8 %copy.9 = bf16[32,6144]{1,0:T(8,128)(2,1)} copy(bf16[32,6144]{1,0:T(8,128)(2,1)} %shard_map.73) | data formatting | bytes 786432

commit v3 on v2

--- a/solution.py
+++ b/solution.py
@@ -16,7 +16,7 @@
 def kernel(
     nspan, nseq,
     level_ref, lo_ref, len_ref, x_ref, mod_ref, w_hbm, wo_hbm, out_ref,
-    w, wo, xg, proj, win_out, win_in, att, acc, mx, den, term, sib, from_low, from_high, fwd, total,
+    w, wo, xg, proj, keys_in, att, acc, mx, den, term, sib, from_low, from_high, fwd, total,
     w_sem, wo_sem,
     g_send_up, g_send_down, g_send_sib, g_recv_z, g_recv_sib,
     k_send, k_recv,
@@ -32,7 +32,6 @@
     chunk = 2 * rows
     wdev = w.shape[2]
     heads = wdev // HD
-    half = tok // 2
     up, down, other = seq + 2, seq - 2, 2 * z + 1 - core
     has_up, has_down = z < nz - 1, z > 0
 
@@ -105,6 +104,22 @@
         at = 2 * oz + part
         return g_copy(2 * oz + 1 - core, part, other, g_send_sib.at[at], g_recv_sib.at[at])
 
+    def k_copy(i, oz):
+        return pltpu.make_async_remote_copy(
+            src_ref=proj.at[pl.ds(1, 2), chunk_rows(oz), :],
+            dst_ref=keys_in.at[span, :, chunk_rows(oz), :],
+            send_sem=k_send.at[i * nz + oz], recv_sem=k_recv.at[span * nz + oz],
+            device_id=(i, seq), device_id_type=MESH,
+        )
+
+    def k_copy_in(i, oz):
+        return pltpu.make_async_remote_copy(
+            src_ref=proj.at[pl.ds(1, 2), chunk_rows(oz), :],
+            dst_ref=keys_in.at[i, :, chunk_rows(oz), :],
+            send_sem=k_send.at[i * nz + oz], recv_sem=k_recv.at[i * nz + oz],
+            device_id=(i, seq), device_id_type=MESH,
+        )
+
     def gather_step(k, carry):
         low, high = z - k, z + k
 
@@ -152,7 +167,14 @@
                     ).astype(BF16)
                     return cc
 
-                lax.fori_loop(0, 3, part, 0)
+                lax.fori_loop(1, 3, part, 0)
+
+                def send_keys(i, cc):
+                    k_copy(i, oz).start()
+                    return cc
+
+                lax.fori_loop(span + 1, nspan, send_keys, 0)
+                lax.fori_loop(0, 1, part, 0)
 
             return c
 
@@ -160,32 +182,6 @@
         return carry
 
     lax.fori_loop(0, nz, gather_step, 0)
-
-    def k_copy(i):
-        return pltpu.make_async_remote_copy(
-            src_ref=win_out.at[i], dst_ref=win_in.at[span],
-            send_sem=k_send.at[i], recv_sem=k_recv.at[span],
-            device_id=(i, seq), device_id_type=MESH,
-        )
-
-    def k_copy_in(i):
-        return pltpu.make_async_remote_copy(
-            src_ref=win_out.at[i], dst_ref=win_in.at[i],
-            send_sem=k_send.at[i], recv_sem=k_recv.at[i],
-            device_id=(i, seq), device_id_type=MESH,
-        )
-
-    def send_window(i, carry):
-        first = lo_ref[i, span]
-        row = lax.broadcasted_iota(jnp.int32, (half, tok), 0)
-        col = lax.broadcasted_iota(jnp.int32, (half, tok), 1)
-        pick = jnp.where(col == row + first, 1.0, 0.0).astype(BF16)
-        for p in range(2):
-            win_out[i, p] = jnp.dot(pick, proj[p + 1], preferred_element_type=F32).astype(BF16)
-        k_copy(i).start()
-        return carry
-
-    lax.fori_loop(span + 1, nspan, send_window, 0)
 
     scale = HD ** (-0.5)
     trans = (((1,), (1,)), ((), ()))
@@ -201,8 +197,11 @@
         acc[h] = jnp.dot(e.astype(BF16), proj[2, :, cols], preferred_element_type=F32)
 
     def await_window(j, carry):
-        k_copy_in(j).wait_recv()
-        return carry
+        def one(oz, c):
+            k_copy_in(j, oz).wait_recv()
+            return c
+
+        return lax.fori_loop(0, nz, one, carry)
 
     lax.fori_loop(0, span, await_window, 0)
 
@@ -219,11 +218,12 @@
         mine = chunk_rows(d)
 
         def see_window(j, carry):
-            seen = lax.broadcasted_iota(jnp.int32, (chunk, half), 1) < len_ref[span, j]
+            offset = lax.broadcasted_iota(jnp.int32, (chunk, tok), 1) - lo_ref[span, j]
+            seen = (offset >= 0) & (offset < len_ref[span, j])
             for h in range(heads):
                 cols = slice(h * HD, (h + 1) * HD)
                 s = lax.dot_general(
-                    proj[0, mine, cols], win_in[j, 0, :, cols], trans,
+                    proj[0, mine, cols], keys_in[j, 0, :, cols], trans,
                     preferred_element_type=F32,
                 ) * scale
                 s = jnp.where(seen, s, -1e30)
@@ -234,7 +234,7 @@
                 mx[h, mine, :] = new
                 den[h, mine, :] = den[h, mine, :] * factor + jnp.sum(e, axis=-1, keepdims=True)
                 acc[h, mine, :] = acc[h, mine, :] * factor + jnp.dot(
-                    e.astype(BF16), win_in[j, 1, :, cols], preferred_element_type=F32
+                    e.astype(BF16), keys_in[j, 1, :, cols], preferred_element_type=F32
                 )
             return carry
 
@@ -353,8 +353,11 @@
     lax.fori_loop(0, nz, drain, 0)
 
     def drain_window(i, carry):
-        k_copy(i).wait_send()
-        return carry
+        def one(oz, c):
+            k_copy(i, oz).wait_send()
+            return c
+
+        return lax.fori_loop(0, nz, one, carry)
 
     lax.fori_loop(span + 1, nspan, drain_window, 0)
 
@@ -379,8 +382,7 @@
             pltpu.VMEM((wdev, width), BF16),
             pltpu.VMEM((tok, width), BF16),
             pltpu.VMEM((3, tok, wdev), BF16),
-            pltpu.VMEM((nspan, 2, tok // 2, wdev), BF16),
-            pltpu.VMEM((nspan, 2, tok // 2, wdev), BF16),
+            pltpu.VMEM((nspan, 2, tok, wdev), BF16),
             pltpu.VMEM((tok, wdev), BF16),
             pltpu.VMEM((heads, tok, HD), F32),
             pltpu.VMEM((heads, tok, HD), F32),
@@ -393,7 +395,7 @@
             pltpu.VMEM((rows, width), F32),
             dma((3,)), dma(()),
             dma((2 * nz,)), dma((2 * nz,)), dma((2 * nz,)), dma((2 * nz,)), dma((2 * nz,)),
-            dma((nspan,)), dma((nspan,)),
+            dma((nspan * nz,)), dma((nspan * nz,)),
             dma((2 * nz,)), dma((nz,)), dma((2 * nz,)), dma((2 * nz,)), dma((nz,)),
         ],
         compiler_params=pltpu.CompilerParams(

time: 90.6 us -> 83.8 us (0.925)
  Pallas kernels: 88.6 us -> 81.9 us
    pallas_call x1, Pallas kernels: 88.6 us -> 81.9 us  [local(): pl.pallas_call(functools.partial(kernel, nspan, nseq), out_shape=jax.Shap...]
where the time goes in v3:
time: 83.8 us; the launch traced here: 83.6 us
  Pallas kernels  81.9 us (98%)
  local copies, waits for them, and re-layouts  1.77 us (2%)
    pallas_call x1, Pallas kernels, local(): pl.pallas_call(functools.partial(kernel, nspan, nseq), out_shape=jax.Shap...  81.9 us
    unnamed x1, local copies, waits for them, and re-layouts  1.77 us

profile of v3, /device:TPU:7, one launch (start us, length us, event | category | flops | bytes accessed | tf_op | source)
XLA Modules:
  0.0 83.6 jit_solution(12438191340092960592)
XLA Ops:
  0.0 81.9 %shard_map.73 = bf16[32,6144]{1,0:T(8,128)(2,1)} custom-call(s32[4]{0:T(128)} %level_ref.1, s32[4,4]{1,0:T(4,128)} %lo_ref.1, s32[4,4]{1,0:T(4,128)} %len_ref.1, bf16[32,6144]{1,0:T(8,128)(2,1)} %x_ref.1, bf16[16,2,6144]{2,1,0:T(2,128)(2,1)} %mod_ref.1, bf16[3,6144,512]{2,1,0:T(8,128)(2,1)} %bitcast.1, bf16[512,6144]{1,0:T(8,128)(2,1)} %wo_hbm.1), custom_call_target="tpu_custom_call" | custom-call | tf_op jit(solution)/shard_map/pallas_call | solution.py:375
  81.9 1.8 %copy.9 = bf16[32,6144]{1,0:T(8,128)(2,1)} copy(bf16[32,6144]{1,0:T(8,128)(2,1)} %shard_map.73) | data formatting | bytes 786432
